TPU v7x, 256 devices: a whole 4x4x8 slice. The times are simulated.
256 devices in a mesh: dp: 16 (over z, core), context: 16 (over x, y).
Axes of the slice: x: 4, y: 4, z: 8, core: 2. Of those that a mesh axis runs over, the one named last changes fastest.
Arguments:
- layer_input: bfloat16 [16, 2048, 8192], P('dp', 'context'), may hold values from -150 to 150
- value_weight: bfloat16 [8192, 512], replicated, may hold values from -0.0625 to 0.0625
- queries: bfloat16 [16, 2048, 4096], P('dp', 'context'), may hold values from -150 to 150
- key_states: bfloat16 [16, 2048, 512], P('dp', 'context'), may hold values from -6 to 6
- out_grads: bfloat16 [16, 2048, 4096], P('dp', 'context'), may hold values from -16 to 16
- lengths: int32 [16], P('dp'), may hold values from 0 to 2048, as said below
Outputs:
- clipped_sum: float32 [8192, 512], P('context', 'dp')
- doc_norms: float32 [16], P('dp')
- key_grads: bfloat16 [16, 2048, 512], P('dp', 'context')
Inputs may be any that keep to these rules, and one draw needn't show every extreme that they name: `lengths`: a slot's document fills the slot's first positions; in every draw some slot is empty and some slot is full.
All inputs are finite; a program needn't handle non-finite values.
Results may differ from a plain program's by a relative error of at most 0.02.
Values may be sent and summed in bfloat16 or wider, within the bound.
A program may use at most 128 MiB of HBM per device.

v0:
```python
import math

import jax
import jax.numpy as jnp
from jax import lax
from jax.sharding import PartitionSpec as P

D = 8192
HD = 128
QH = 32
KVH = 4


def attend_block(query_block, grad_block, keys_all, values_all, block_start, length):
    softmax_scale = HD ** (-0.5)
    block_rows = query_block.shape[0]
    seq_total = keys_all.shape[0]
    query_pos = block_start + lax.iota(jnp.int32, block_rows)
    key_pos = lax.iota(jnp.int32, seq_total)
    grad_block = jnp.where(
        (query_pos < length)[:, None, None], grad_block, jnp.zeros_like(grad_block)
    )
    scores = (
        jnp.einsum("ihd,jd->hij", query_block, keys_all, preferred_element_type=jnp.float32)
        * softmax_scale
    )
    scores = jnp.where((query_pos[:, None] >= key_pos[None, :])[None], scores, -jnp.inf)
    row_peak = jnp.max(scores, axis=-1, keepdims=True)
    weights = jnp.exp(scores - row_peak)
    weights = weights / jnp.sum(weights, axis=-1, keepdims=True)
    probs_low = weights.astype(jnp.bfloat16)
    attended = jnp.einsum("hij,jd->hid", probs_low, values_all, preferred_element_type=jnp.float32)
    grad_heads = jnp.transpose(grad_block, (1, 0, 2))
    offsets = jnp.sum(grad_heads.astype(jnp.float32) * attended, axis=-1)
    grad_probs = jnp.einsum(
        "hid,jd->hij", grad_heads, values_all, preferred_element_type=jnp.float32
    )
    grad_scores = (weights * (grad_probs - offsets[..., None])).astype(jnp.bfloat16)
    key_part = (
        jnp.einsum("hij,ihd->jhd", grad_scores, query_block, preferred_element_type=jnp.float32)
        * softmax_scale
    )
    value_part = jnp.einsum(
        "hij,hid->jhd", probs_low, grad_heads, preferred_element_type=jnp.float32
    )
    return (key_part, value_part)


def body(layer_input, value_weight, queries, key_states, out_grads, lengths):
    context_size = lax.axis_size("context")
    local_rows = layer_input.shape[1]
    local_heads = QH // context_size
    seq_total = local_rows * context_size
    block_rows = min(512, seq_total)
    length = lengths[0]
    values = jnp.dot(layer_input[0], value_weight, preferred_element_type=jnp.float32).astype(
        jnp.bfloat16
    )

    def spread(states):
        return jnp.repeat(states.reshape(local_rows, KVH, HD), context_size // KVH, axis=1)

    key_heads, value_heads = (
        lax.all_to_all(spread(key_states[0]), "context", split_axis=1, concat_axis=0, tiled=True),
        lax.all_to_all(spread(values), "context", split_axis=1, concat_axis=0, tiled=True),
    )
    keys_all = key_heads[:, 0]
    values_all = value_heads[:, 0]
    block_count = seq_total // block_rows
    query_split = queries[0].reshape(local_rows, context_size, local_heads, HD)
    grad_split = out_grads[0].reshape(local_rows, context_size, local_heads, HD)
    query_all = lax.all_to_all(query_split, "context", split_axis=1, concat_axis=0, tiled=True)[
        :, 0
    ]
    grad_all = lax.all_to_all(grad_split, "context", split_axis=1, concat_axis=0, tiled=True)[:, 0]
    head_count = query_all.shape[1]

    def one_block(block_index, running):
        block_start = block_index * block_rows
        query_block = lax.dynamic_slice_in_dim(query_all, block_start, block_rows, 0)
        grad_block = lax.dynamic_slice_in_dim(grad_all, block_start, block_rows, 0)
        key_part, value_part = attend_block(
            query_block, grad_block, keys_all, values_all, block_start, length
        )
        return (running[0] + key_part, running[1] + value_part)

    zeros_heads = jnp.zeros((seq_total, head_count, HD), jnp.float32)
    key_grad, value_grad = lax.fori_loop(0, block_count, one_block, (zeros_heads, zeros_heads))
    key_grad, value_grad = (key_grad[:, None], value_grad[:, None])
    key_back, value_back = (
        lax.all_to_all(key_grad, "context", split_axis=0, concat_axis=1, tiled=True),
        lax.all_to_all(value_grad, "context", split_axis=0, concat_axis=1, tiled=True),
    )
    key_sum = jnp.sum(key_back.reshape(local_rows, KVH, QH // KVH, HD), axis=2)
    value_sum = jnp.sum(value_back.reshape(local_rows, KVH, QH // KVH, HD), axis=2)
    key_grads = key_sum.reshape(1, local_rows, KVH * HD).astype(jnp.bfloat16)
    value_low = value_sum.reshape(local_rows, KVH * HD).astype(jnp.bfloat16)
    contract_rows = (((0,), (0,)), ((), ()))
    input_part = layer_input[0]
    own_grad = lax.psum_scatter(
        lax.dot_general(
            input_part, value_low, contract_rows, preferred_element_type=jnp.float32
        ).astype(jnp.bfloat16),
        "context",
        scatter_dimension=0,
        tiled=True,
    ).astype(jnp.float32)
    partial_value = jnp.sum(own_grad * own_grad)
    total_squares = lax.psum(partial_value, "context")
    doc_norm = jnp.sqrt(total_squares)
    factor = math.sqrt(D * KVH * HD) / (doc_norm + 0.01)
    clipped = lax.psum_scatter(
        (own_grad * factor).astype(jnp.bfloat16), "dp", scatter_dimension=1, tiled=True
    ).astype(jnp.float32)
    return (clipped, doc_norm.reshape(1), key_grads)


def solution(mesh):
    placed = (
        P("dp", "context", None),
        P(),
        P("dp", "context", None),
        P("dp", "context", None),
        P("dp", "context", None),
        P("dp"),
    )
    return jax.shard_map(
        body,
        mesh=mesh,
        in_specs=placed,
        out_specs=(P("context", "dp"), P("dp"), P("dp", "context", None)),
        check_vma=False,
    )
```

profile of v0, /device:TPU:1, one launch (start us, length us, event | category | flops | bytes accessed | tf_op | source)
XLA Modules:
  0.0 471.8 jit_solution(8661934245471723993)
XLA Ops:
  7.2 1.6 copy-done
  8.8 4.6 fusion.50
  13.5 0.9 broadcast_in_dim.82
  14.5 7.6 %all-to-all-start.3 = ((bf16[128,16,128]{0,2,1:T(8,128)(2,1)}), bf16[128,16,128]{0,2,1:T(8,128)(2,1)}, u32[]{:S(2)}, u32[]{:S(2)}) async-start(bf16[128,16,128]{0,2,1:T(8,128)(2,1)} %bitcast.15), calls=%async_computation.3 | async-start | bytes 1048576 | tf_op jit(solution)/shard_map/all_to_all | solution.py:65
  22.1 1.6 copy.55
  23.7 1.3 copy.56
  25.1 7.4 %all-to-all-done.3 = bf16[128,16,128]{0,2,1:T(8,128)(2,1)} async-done(((bf16[128,16,128]{0,2,1:T(8,128)(2,1)}), bf16[128,16,128]{0,2,1:T(8,128)(2,1)}, u32[]{:S(2)}, u32[]{:S(2)}) %all-to-all-start.3) | async-done | bytes 524320 | tf_op jit(solution)/shard_map/all_to_all | solution.py:65
  32.5 3.7 all-to-all-start
  36.1 2.3 copy.59
  38.4 12.4 %all-to-all-done = bf16[128,16,2,128]{3,0,2,1:T(8,128)(2,1)S(1)} async-done(((bf16[128,16,2,128]{3,0,2,1:T(8,128)(2,1)}), bf16[128,16,2,128]{3,0,2,1:T(8,128)(2,1)S(1)}, u32[]{:S(2)}, u32[]{:S(2)}) %all-to-all-start) | async-done | bytes 1048608 | tf_op jit(solution)/shard_map/all_to_all | solution.py:72
  50.9 4.6 all-to-all-start.2
  55.5 14.2 %all-to-all-done.2 = bf16[128,16,2,128]{0,3,2,1:T(8,128)(2,1)} async-done(((bf16[128,16,2,128]{0,3,2,1:T(8,128)(2,1)}), bf16[128,16,2,128]{0,3,2,1:T(8,128)(2,1)}, u32[]{:S(2)}, u32[]{:S(2)}) %all-to-all-start.2) | async-done | bytes 1048608 | tf_op jit(solution)/shard_map/all_to_all | solution.py:75
  69.8 0.9 broadcast_in_dim.81
  70.7 5.2 %all-to-all-start.1 = ((bf16[128,16,128]{2,0,1:T(8,128)(2,1)}), bf16[128,16,128]{2,0,1:T(8,128)(2,1)}, u32[]{:S(2)}, u32[]{:S(2)}) async-start(bf16[128,16,128]{2,0,1:T(8,128)(2,1)} %bitcast.331), calls=%async_computation.1 | async-start | bytes 1048576 | tf_op jit(solution)/shard_map/all_to_all | solution.py:64
  76.1 2.1 copy.62
  78.2 2.1 copy.64
  80.2 1.1 copy.57
  81.3 2.3 copy.60
  83.6 1.3 all-to-all-done.1
  84.9 122.1 %while.16 = (s32[]{:T(128)}, f32[2048,2,128]{0,2,1:T(8,128)}, f32[2048,2,128]{0,2,1:T(8,128)}, bf16[2048,2,128]{2,0,1:T(8,128)(2,1)}, bf16[2048,128]{1,0:T(8,128...) while((s32[]{:T(128)}, f32[2048,2,128]{0,2,1:T(8,128)}, ...), condition=%wide.region_4.5_spmd.clone, body=%wide.region_0.4_spmd.clone.sunk | while | flops 2709785088 | bytes 71067904 | solution.py:88
  84.9 0.7 iota_compare_fusion.2
  85.6 7.4 %fusion.91 = (f32[2,512]{1,0:T(2,128)S(1)}, f32[2,512,2048]{2,1,0:T(8,128)}) fusion(pred[512,2048]{1,0:T(8,128)(4,1)S(1)} %iota_compare_fusion.2, bf16[2048,128]{1,0:T(8,128)(2,1)} %get-tuple-element.298, bf16[2048,2,128]{2,0,1:T(8,128)(2,1)} %get-tuple-element.297, s32[]{:T(128)S(6)} %select_n.62), kind=kOutput, calls=%fused_computation.54.clone.1 | convolution fusion | flops 545261568 | bytes 10227716 | tf_op jit(solution)/shard_map/while/body/eval_jaxpr/sub | solution.py:29
  92.9 6.6 %fusion.92 = bf16[2,512,2048]{2,1,0:T(8,128)(2,1)} fusion(f32[2,512,2048]{2,1,0:T(8,128)} %get-tuple-element.268, f32[2,512]{1,0:T(2,128)S(1)} %get-tuple-element.269), kind=kLoop, calls=%fused_computation.12.clone.1 | loop fusion | flops 4194304 | bytes 12587008 | tf_op jit(solution)/shard_map/while/body/eval_jaxpr/convert_element_type | solution.py:31
  99.5 1.0 constant_dynamic-slice_fusion.2
  100.7 0.7 broadcast_compare_fusion.2
  101.3 4.4 fusion.95
  105.8 1.5 fusion.93
  107.3 7.2 %fusion.94 = f32[2048,2,128]{0,2,1:T(8,128)} fusion(f32[2048,2,128]{0,2,1:T(8,128)} %get-tuple-element.283, f32[2,512]{1,0:T(2,128)S(1)} %fusion.93, f32[2,512,2048]{2,1,0:T(8,128)} %get-tuple-element.268, f32[2,512]{1,0:T(2,128)S(1)} %get-tuple-element.269, pred[]{:T(512)S(6)} %compare.3, bf16[2048,128]{0,1:T(8,128)(2,1)S(1)} %copy-done.2, ...), kind=kOutput, calls=%fused_computation.17.clone.1 | convolution fusion | flops 1083834368 | bytes 13640197 | tf_op jit(solution)/shard_map/while/body/eval_jaxpr/hij,ihd->jhd/dot_general | solution.py:40
  115.1 7.4 %fusion.91 = (f32[2,512]{1,0:T(2,128)S(1)}, f32[2,512,2048]{2,1,0:T(8,128)}) fusion(pred[512,2048]{1,0:T(8,128)(4,1)S(1)} %iota_compare_fusion.2, bf16[2048,128]{1,0:T(8,128)(2,1)} %get-tuple-element.298, bf16[2048,2,128]{2,0,1:T(8,128)(2,1)} %get-tuple-element.297, s32[]{:T(128)S(6)} %select_n.62), kind=kOutput, calls=%fused_computation.54.clone.1 | convolution fusion | flops 545261568 | bytes 10227716 | tf_op jit(solution)/shard_map/while/body/eval_jaxpr/sub | solution.py:29
  122.5 6.6 %fusion.92 = bf16[2,512,2048]{2,1,0:T(8,128)(2,1)} fusion(f32[2,512,2048]{2,1,0:T(8,128)} %get-tuple-element.268, f32[2,512]{1,0:T(2,128)S(1)} %get-tuple-element.269), kind=kLoop, calls=%fused_computation.12.clone.1 | loop fusion | flops 4194304 | bytes 12587008 | tf_op jit(solution)/shard_map/while/body/eval_jaxpr/convert_element_type | solution.py:31
  129.1 1.0 constant_dynamic-slice_fusion.2
  130.9 5.1 %fusion.95 = f32[2048,2,128]{0,2,1:T(8,128)} fusion(bf16[2,512,2048]{2,1,0:T(8,128)(2,1)} %fusion.92, f32[2048,2,128]{0,2,1:T(8,128)} %get-tuple-element.284, pred[]{:T(512)S(6)} %compare.3, bf16[512,2,128]{0,2,1:T(8,128)(2,1)S(1)} %copy.187, pred[512]{0:T(512)(128)(4,1)S(1)} %broadcast_compare_fusion.2), kind=kOutput, calls=%fused_computation.14.clone.1 | convolution fusion | flops 538050560 | bytes 8651265 | tf_op jit(solution)/shard_map/while/body/eval_jaxpr/hij,hid->jhd/dot_general | solution.py:43
  136.0 1.5 fusion.93
  137.5 7.8 %fusion.94 = f32[2048,2,128]{0,2,1:T(8,128)} fusion(f32[2048,2,128]{0,2,1:T(8,128)} %get-tuple-element.283, f32[2,512]{1,0:T(2,128)S(1)} %fusion.93, f32[2,512,2048]{2,1,0:T(8,128)} %get-tuple-element.268, f32[2,512]{1,0:T(2,128)S(1)} %get-tuple-element.269, pred[]{:T(512)S(6)} %compare.3, bf16[2048,128]{0,1:T(8,128)(2,1)S(1)} %copy-done.2, ...), kind=kOutput, calls=%fused_computation.17.clone.1 | convolution fusion | flops 1083834368 | bytes 13640197 | tf_op jit(solution)/shard_map/while/body/eval_jaxpr/hij,ihd->jhd/dot_general | solution.py:40
  146.0 7.4 %fusion.91 = (f32[2,512]{1,0:T(2,128)S(1)}, f32[2,512,2048]{2,1,0:T(8,128)}) fusion(pred[512,2048]{1,0:T(8,128)(4,1)S(1)} %iota_compare_fusion.2, bf16[2048,128]{1,0:T(8,128)(2,1)} %get-tuple-element.298, bf16[2048,2,128]{2,0,1:T(8,128)(2,1)} %get-tuple-element.297, s32[]{:T(128)S(6)} %select_n.62), kind=kOutput, calls=%fused_computation.54.clone.1 | convolution fusion | flops 545261568 | bytes 10227716 | tf_op jit(solution)/shard_map/while/body/eval_jaxpr/sub | solution.py:29
  153.4 6.6 %fusion.92 = bf16[2,512,2048]{2,1,0:T(8,128)(2,1)} fusion(f32[2,512,2048]{2,1,0:T(8,128)} %get-tuple-element.268, f32[2,512]{1,0:T(2,128)S(1)} %get-tuple-element.269), kind=kLoop, calls=%fused_computation.12.clone.1 | loop fusion | flops 4194304 | bytes 12587008 | tf_op jit(solution)/shard_map/while/body/eval_jaxpr/convert_element_type | solution.py:31
  159.9 1.0 constant_dynamic-slice_fusion.2
  161.8 5.1 %fusion.95 = f32[2048,2,128]{0,2,1:T(8,128)} fusion(bf16[2,512,2048]{2,1,0:T(8,128)(2,1)} %fusion.92, f32[2048,2,128]{0,2,1:T(8,128)} %get-tuple-element.284, pred[]{:T(512)S(6)} %compare.3, bf16[512,2,128]{0,2,1:T(8,128)(2,1)S(1)} %copy.187, pred[512]{0:T(512)(128)(4,1)S(1)} %broadcast_compare_fusion.2), kind=kOutput, calls=%fused_computation.14.clone.1 | convolution fusion | flops 538050560 | bytes 8651265 | tf_op jit(solution)/shard_map/while/body/eval_jaxpr/hij,hid->jhd/dot_general | solution.py:43
  166.8 1.5 fusion.93
  168.4 7.8 %fusion.94 = f32[2048,2,128]{0,2,1:T(8,128)} fusion(f32[2048,2,128]{0,2,1:T(8,128)} %get-tuple-element.283, f32[2,512]{1,0:T(2,128)S(1)} %fusion.93, f32[2,512,2048]{2,1,0:T(8,128)} %get-tuple-element.268, f32[2,512]{1,0:T(2,128)S(1)} %get-tuple-element.269, pred[]{:T(512)S(6)} %compare.3, bf16[2048,128]{0,1:T(8,128)(2,1)S(1)} %copy-done.2, ...), kind=kOutput, calls=%fused_computation.17.clone.1 | convolution fusion | flops 1083834368 | bytes 13640197 | tf_op jit(solution)/shard_map/while/body/eval_jaxpr/hij,ihd->jhd/dot_general | solution.py:40
  176.8 7.4 %fusion.91 = (f32[2,512]{1,0:T(2,128)S(1)}, f32[2,512,2048]{2,1,0:T(8,128)}) fusion(pred[512,2048]{1,0:T(8,128)(4,1)S(1)} %iota_compare_fusion.2, bf16[2048,128]{1,0:T(8,128)(2,1)} %get-tuple-element.298, bf16[2048,2,128]{2,0,1:T(8,128)(2,1)} %get-tuple-element.297, s32[]{:T(128)S(6)} %select_n.62), kind=kOutput, calls=%fused_computation.54.clone.1 | convolution fusion | flops 545261568 | bytes 10227716 | tf_op jit(solution)/shard_map/while/body/eval_jaxpr/sub | solution.py:29
  184.2 6.6 %fusion.92 = bf16[2,512,2048]{2,1,0:T(8,128)(2,1)} fusion(f32[2,512,2048]{2,1,0:T(8,128)} %get-tuple-element.268, f32[2,512]{1,0:T(2,128)S(1)} %get-tuple-element.269), kind=kLoop, calls=%fused_computation.12.clone.1 | loop fusion | flops 4194304 | bytes 12587008 | tf_op jit(solution)/shard_map/while/body/eval_jaxpr/convert_element_type | solution.py:31
  190.8 1.0 constant_dynamic-slice_fusion.2
  192.6 5.1 %fusion.95 = f32[2048,2,128]{0,2,1:T(8,128)} fusion(bf16[2,512,2048]{2,1,0:T(8,128)(2,1)} %fusion.92, f32[2048,2,128]{0,2,1:T(8,128)} %get-tuple-element.284, pred[]{:T(512)S(6)} %compare.3, bf16[512,2,128]{0,2,1:T(8,128)(2,1)S(1)} %copy.187, pred[512]{0:T(512)(128)(4,1)S(1)} %broadcast_compare_fusion.2), kind=kOutput, calls=%fused_computation.14.clone.1 | convolution fusion | flops 538050560 | bytes 8651265 | tf_op jit(solution)/shard_map/while/body/eval_jaxpr/hij,hid->jhd/dot_general | solution.py:43
  197.7 1.5 fusion.93
  199.2 7.8 %fusion.94 = f32[2048,2,128]{0,2,1:T(8,128)} fusion(f32[2048,2,128]{0,2,1:T(8,128)} %get-tuple-element.283, f32[2,512]{1,0:T(2,128)S(1)} %fusion.93, f32[2,512,2048]{2,1,0:T(8,128)} %get-tuple-element.268, f32[2,512]{1,0:T(2,128)S(1)} %get-tuple-element.269, pred[]{:T(512)S(6)} %compare.3, bf16[2048,128]{0,1:T(8,128)(2,1)S(1)} %copy-done.2, ...), kind=kOutput, calls=%fused_computation.17.clone.1 | convolution fusion | flops 1083834368 | bytes 13640197 | tf_op jit(solution)/shard_map/while/body/eval_jaxpr/hij,ihd->jhd/dot_general | solution.py:40
  207.0 4.1 copy.65
  211.1 29.9 %all_to_all.78 = f32[2048,1,2,128]{3,2,1,0:T(2,128)} all-to-all(f32[2048,1,2,128]{3,2,1,0:T(2,128)} %bitcast.323), channel_id=1, replica_groups=mesh['dp'=16,'context'=16] {'context'}, dimensions={0} | all-to-all | bytes 4194304 | tf_op jit(solution)/shard_map/all_to_all | solution.py:92
  241.0 8.8 %reduce_sum.75 = f32[2048,128]{1,0:T(8,128)S(1)} reduce(f32[2048,1,2,128]{3,2,1,0:T(2,128)} %all_to_all.78, f32[]{:T(128)} %constant.59.clone.1), dimensions={1,2}, to_apply=%region_5.6 | reduce | flops 262144 | bytes 3145732 | tf_op jit(solution)/shard_map/reduce_sum | solution.py:95
  249.8 1.4 copy.80
  251.2 1.9 reduce_sum.79
  253.2 5.6 %fusion.46 = bf16[8192,512]{0,1:T(8,128)(2,1)} fusion(bf16[128,512]{0,1:T(8,128)(2,1)S(1)} %bitcast.336, bf16[1,128,8192]{2,1,0:T(8,128)(2,1)S(1)} %copy-done), kind=kOutput, calls=%fused_computation.45 | convolution fusion | flops 1077936128 | bytes 10616832 | tf_op jit(solution)/shard_map/dot_general | solution.py:101
  258.8 4.2 copy.68
  262.9 4.4 all-to-all-start.5
  267.4 99.9 %reduce-scatter.3.cloned.1.call-done = bf16[512,512]{0,1:T(8,128)(2,1)} async-done(((bf16[8192,512]{0,1:T(8,128)(2,1)}), bf16[512,512]{0,1:T(8,128)(2,1)}) %reduce-scatter.3.cloned.1.call-update) | async-done | bytes 524304 | tf_op jit(solution)/shard_map/reduce_scatter | solution.py:100
  367.3 1.9 fusion.53
  369.2 32.0 %psum.7 = f32[]{:T(128)} all-reduce(f32[]{:T(128)} %fusion.53), channel_id=1, replica_groups=mesh['dp'=16,'context'=16] {'context'}, use_global_device_ids=true, to_apply=%region_9.10 | all-reduce | flops 1 | bytes 8 | tf_op jit(solution)/shard_map/psum | solution.py:109
  402.0 1.9 fusion.54
  403.9 9.8 %reduce_sum.81 = f32[2048,128]{1,0:T(8,128)} reduce(f32[2048,1,2,128]{3,2,1,0:T(2,128)} %all-to-all-done.5, f32[]{:T(128)} %constant.59.clone.1), dimensions={1,2}, to_apply=%region_11.12 | reduce | flops 262144 | bytes 3145732 | tf_op jit(solution)/shard_map/reduce_sum | solution.py:94
  413.8 1.7 copy.82
  415.5 0.7 reduce_sum.85
  416.3 0.8 copy.71
  417.0 45.4 %reduce-scatter.5.cloned.1.call-done = bf16[512,32]{0,1:T(8,128)(2,1)} async-done(((bf16[512,512]{0,1:T(8,128)(2,1)}), bf16[512,32]{0,1:T(8,128)(2,1)}) %reduce-scatter.5.cloned.1.call-update) | async-done | bytes 32784 | tf_op jit(solution)/shard_map/reduce_scatter | solution.py:112
  462.5 1.4 convert_element_type.72
  (45 shorter events, 5.1 us)
Async XLA Ops:
  7.2 1.6 copy-start
  14.5 18.0 %all-to-all-start.3 = ((bf16[128,16,128]{0,2,1:T(8,128)(2,1)}), bf16[128,16,128]{0,2,1:T(8,128)(2,1)}, u32[]{:S(2)}, u32[]{:S(2)}) async-start(bf16[128,16,128]{0,2,1:T(8,128)(2,1)} %bitcast.15), calls=%async_computation.3 | async-start | bytes 1048576 | tf_op jit(solution)/shard_map/all_to_all | solution.py:65
  23.7 31.7 %copy-start.3 = (bf16[1,128,512]{2,1,0:T(8,128)(2,1)S(1)}, bf16[1,128,512]{2,1,0:T(8,128)(2,1)}, u32[]{:S(2)}) copy-start(bf16[1,128,512]{2,1,0:T(8,128)(2,1)} %param.11) | copy-start | bytes 393220
  32.5 18.4 %all-to-all-start = ((bf16[128,16,2,128]{3,0,2,1:T(8,128)(2,1)}), bf16[128,16,2,128]{3,0,2,1:T(8,128)(2,1)S(1)}, u32[]{:S(2)}, u32[]{:S(2)}) async-start(bf16[128,16,2,128]{3,0,2,1:T(8,128)(2,1)} %copy.56), calls=%async_computation | async-start | bytes 2097152 | tf_op jit(solution)/shard_map/all_to_all | solution.py:72
  50.9 18.9 %all-to-all-start.2 = ((bf16[128,16,2,128]{0,3,2,1:T(8,128)(2,1)}), bf16[128,16,2,128]{0,3,2,1:T(8,128)(2,1)}, u32[]{:S(2)}, u32[]{:S(2)}) async-start(bf16[128,16,2,128]{0,3,2,1:T(8,128)(2,1)} %bitcast.325), calls=%async_computation.2 | async-start | bytes 2097152 | tf_op jit(solution)/shard_map/all_to_all | solution.py:75
  70.7 14.2 %all-to-all-start.1 = ((bf16[128,16,128]{2,0,1:T(8,128)(2,1)}), bf16[128,16,128]{2,0,1:T(8,128)(2,1)}, u32[]{:S(2)}, u32[]{:S(2)}) async-start(bf16[128,16,128]{2,0,1:T(8,128)(2,1)} %bitcast.331), calls=%async_computation.1 | async-start | bytes 1048576 | tf_op jit(solution)/shard_map/all_to_all | solution.py:64
  75.9 291.4 %reduce-scatter.3.cloned.1.call-start = ((), (), s32[]{:S(2)}) async-start(), calls=%async_computation.8 | async-start | bytes 8912896 | tf_op jit(solution)/shard_map/reduce_scatter | solution.py:100
  101.3 4.4 copy-start.1
  101.3 4.4 copy-start.2
  130.9 5.1 %copy-start.1 = (bf16[2,512,2048]{2,1,0:T(8,128)(2,1)S(1)}, bf16[2,512,2048]{2,1,0:T(8,128)(2,1)}, u32[]{:S(2)}) copy-start(bf16[2,512,2048]{2,1,0:T(8,128)(2,1)} %fusion.92) | copy-start | bytes 12582916 | tf_op jit(solution)/shard_map/while
  130.9 5.1 %copy-start.2 = (bf16[2048,128]{0,1:T(8,128)(2,1)S(1)}, bf16[2048,128]{0,1:T(8,128)(2,1)}, u32[]{:S(2)}) copy-start(bf16[2048,128]{0,1:T(8,128)(2,1)} %get-tuple-element.301) | copy-start | bytes 1572868 | tf_op jit(solution)/shard_map/while
  161.7 5.1 %copy-start.1 = (bf16[2,512,2048]{2,1,0:T(8,128)(2,1)S(1)}, bf16[2,512,2048]{2,1,0:T(8,128)(2,1)}, u32[]{:S(2)}) copy-start(bf16[2,512,2048]{2,1,0:T(8,128)(2,1)} %fusion.92) | copy-start | bytes 12582916 | tf_op jit(solution)/shard_map/while
  161.7 5.1 %copy-start.2 = (bf16[2048,128]{0,1:T(8,128)(2,1)S(1)}, bf16[2048,128]{0,1:T(8,128)(2,1)}, u32[]{:S(2)}) copy-start(bf16[2048,128]{0,1:T(8,128)(2,1)} %get-tuple-element.301) | copy-start | bytes 1572868 | tf_op jit(solution)/shard_map/while
  192.6 5.1 %copy-start.1 = (bf16[2,512,2048]{2,1,0:T(8,128)(2,1)S(1)}, bf16[2,512,2048]{2,1,0:T(8,128)(2,1)}, u32[]{:S(2)}) copy-start(bf16[2,512,2048]{2,1,0:T(8,128)(2,1)} %fusion.92) | copy-start | bytes 12582916 | tf_op jit(solution)/shard_map/while
  192.6 5.1 %copy-start.2 = (bf16[2048,128]{0,1:T(8,128)(2,1)S(1)}, bf16[2048,128]{0,1:T(8,128)(2,1)}, u32[]{:S(2)}) copy-start(bf16[2048,128]{0,1:T(8,128)(2,1)} %get-tuple-element.301) | copy-start | bytes 1572868 | tf_op jit(solution)/shard_map/while
  262.9 141.0 %all-to-all-start.5 = ((f32[2048,1,2,128]{3,2,1,0:T(2,128)}), f32[2048,1,2,128]{3,2,1,0:T(2,128)}, u32[]{:S(2)}, u32[]{:S(2)}) async-start(f32[2048,1,2,128]{3,2,1,0:T(2,128)} %bitcast.322), calls=%async_computation.7 | async-start | bytes 4194304 | tf_op jit(solution)/shard_map/all_to_all | solution.py:91
  267.4 195.1 %reduce-scatter.5.cloned.1.call-start = ((), (), s32[]{:S(2)}) async-start(), calls=%async_computation.9 | async-start | bytes 557056 | tf_op jit(solution)/shard_map/reduce_scatter | solution.py:112
Sparse Core Ops, SparseCore 0:
  258.9 108.3 reduce-scatter.2
  404.1 58.3 reduce-scatter.4
where the time goes:
time: 476 us; the launch traced here: 472 us
  waiting for transfers between devices  181 us (38%)
  matrix products  96 us (20%)
  blocking collectives  61.9 us (13%)
  other arithmetic  58.1 us (12%)
  local copies, waits for them, and re-layouts  33 us (7%)
  starting transfers between devices  25.7 us (5%)
  between operations  16.1 us (3%)
    reduce_scatter x1, waiting for transfers between devices, body(): lax.psum_scatter(lax.dot_general(input_part, value_low, contract_rows, pr...  99.9 us
    reduce_scatter x1, waiting for transfers between devices, body(): lax.psum_scatter((own_grad * factor).astype(jnp.bfloat16), 'dp', scatter_...  45.4 us
    psum x1, blocking collectives, body(): total_squares = lax.psum(partial_value, 'context')  32 us
    dot_general x4, matrix products, attend_block(): jnp.einsum('hij,ihd->jhd', grad_scores, query_block, preferred_element_ty...  30.5 us
    all_to_all x1, blocking collectives, body(): lax.all_to_all(value_grad, 'context', split_axis=0, concat_axis=1, tiled=...  29.9 us
    sub x4, matrix products, attend_block(): weights = jnp.exp(scores - row_peak)  29.6 us
    convert_element_type x4, other arithmetic, attend_block(): probs_low = weights.astype(jnp.bfloat16)  26.4 us
    dot_general x4, matrix products, attend_block(): jnp.einsum('hij,hid->jhd', probs_low, grad_heads, preferred_element_type=...  19.6 us
  transfers between devices with their start and end apart: 7, of which 6 were waited for; matrix products, arithmetic and copies ran while one was open for 7% of the time, Pallas kernels for 0%

commit v1 on v0

v1 whole, which is shorter than its diff:
```python
import functools
import math

import jax
import jax.numpy as jnp
from jax import lax
from jax.experimental import pallas as pl
from jax.experimental.pallas import tpu as pltpu
from jax.sharding import PartitionSpec as P

MESH = pl.DeviceIdType.MESH
BF = jnp.bfloat16
F32 = jnp.float32

D = 8192
HD = 128
KV = 512
NX = 4
NY = 4
NC = NX * NY
ND = 16
ROWS = 128
GH = 8
GW = GH * HD
SEQ = NC * ROWS
CK = NY * ROWS
KS = 256
STEPS = CK // KS
DB = D // NC
CB = KV // ND
WCH = 8
SCALE = HD ** (-0.5)
C2 = SCALE * math.log2(math.e)
CLIP = math.sqrt(D * KV)

K1, Q, G, K2, V1, V2, RV, RK, KO = range(0, 36, 4)
XT, AG, NM, GR, FC = range(36, 36 + 80, 16)
K2S, V2S, NSEM = 116, 128, 140
LX, LQ, LG, LK, LV, LXG, LW = 0, 1, 2, 3, 4, 5, 6


def attend(k, y, length, qb, gb, kf, vf, dk, dv, qs, gs, qt, gt, p_s, d_s, m_s):
    q_pos = CK * k + ROWS * y + lax.broadcasted_iota(jnp.int32, (ROWS, HD), 0)
    keep = q_pos < length
    for h in range(GH):
        cols = slice(h * HD, (h + 1) * HD)
        q = qb[k, :, cols]
        g = jnp.where(keep, gb[k, :, cols].astype(F32), 0.0)
        qs[cols, :] = q
        gs[cols, :] = g.astype(BF)
        qt[:, cols] = q.astype(F32).T.astype(BF)
        gt[:, cols] = g.T.astype(BF)

    def sweep_a(j, carry, masked):
        m, l, off = carry
        rows = pl.ds(pl.multiple_of(j * KS, KS), KS)
        s = jnp.dot(kf[rows, :], qt[...], preferred_element_type=F32)
        dp = jnp.dot(vf[rows, :], gt[...], preferred_element_type=F32)
        if masked:
            ki = lax.broadcasted_iota(jnp.int32, (KS, GW), 0)
            qi = lax.broadcasted_iota(jnp.int32, (KS, GW), 1) & (HD - 1)
            s = jnp.where(ki - qi <= CK * k + ROWS * y - KS * j, s, -jnp.inf)
        mn = jnp.maximum(m, jnp.max(s, axis=0, keepdims=True))
        a = jnp.exp2((m - mn) * C2)
        p = jnp.exp2((s - mn) * C2)
        p_s[rows, :] = p
        d_s[rows, :] = dp
        m_s[j] = jnp.broadcast_to(mn, (8, GW))
        l = l * a + jnp.sum(p, axis=0, keepdims=True)
        off = off * a + jnp.sum(p * dp, axis=0, keepdims=True)
        return mn, l, off

    zero = jnp.zeros((1, GW), F32)
    carry = (jnp.full((1, GW), -jnp.inf, F32), zero, zero)
    carry = lax.fori_loop(0, k * STEPS, lambda j, c: sweep_a(j, c, False), carry)
    for t in range(STEPS):
        carry = sweep_a(k * STEPS + t, carry, True)
    m, l, off = carry
    inv = 1.0 / l
    off = off * inv

    def sweep_b(j, _):
        rows = pl.ds(pl.multiple_of(j * KS, KS), KS)
        p = p_s[rows, :] * (jnp.exp2((m_s[j][0:1] - m) * C2) * inv)
        ds = p * (d_s[rows, :] - off)
        dv[rows, :] += jnp.dot(p.astype(BF), gs[...], preferred_element_type=F32)
        dk[rows, :] += jnp.dot(ds.astype(BF), qs[...], preferred_element_type=F32)
        return 0

    lax.fori_loop(0, (k + 1) * STEPS, sweep_b, 0)


def kernel(
    len_ref, x_ref, w_ref, q_ref, k_ref, g_ref,
    cs_ref, nm_ref, kg_ref,
    xv, wv, vown, qb, gb, kf, vf, xg, dk, dv, qs, gs, qt, gt, p_s, d_s, m_s,
    dvs, dks, dvr, dkr, kout, kin, dvt, acc, gsend, gr, nsend, nr, fsend, fr,
    send, recv, local,
):
    c = lax.axis_index("context")
    d = lax.axis_index("dp")
    x, y = c // NY, lax.rem(c, NY)
    length = len_ref[0]
    sent = []

    def at_x(o):
        return lax.rem(x + o, NX)

    def at_y(o):
        return lax.rem(y + o, NY)

    def remote(src, dst, sem, **peer):
        copy = pltpu.make_async_remote_copy(
            src_ref=src, dst_ref=dst, send_sem=send.at[sem], recv_sem=recv.at[sem],
            device_id=peer, device_id_type=MESH,
        )
        copy.start()
        sent.append(copy)
        return copy

    def near(src, dst, sem):
        copy = pltpu.make_async_copy(src, dst, local.at[sem])
        copy.start()
        return copy

    def cols(index, width):
        return pl.ds(pl.multiple_of(index * width, width), width)

    def place(ref, xi, yi):
        return ref.at[cols(xi * NY + yi, ROWS), :]

    load_x = near(x_ref, xv, LX)
    load_w = [near(w_ref.at[pl.ds(i * (D // WCH), D // WCH), :], wv.at[i], LW + i) for i in range(WCH)]
    own = [
        near(k_ref.at[:, cols(x, HD)], place(kf, x, y), LK),
        near(q_ref.at[:, cols(x, GW)], qb.at[x], LQ),
        near(g_ref.at[:, cols(x, GW)], gb.at[x], LG),
        near(x_ref.at[:, cols(c, DB)], xg.at[y, cols(x, ROWS), :], LXG),
    ]

    barrier = pltpu.get_barrier_semaphore()
    for i in range(NX):
        for j in range(NY):
            if i or j:
                peer = {"context": at_x(i) * NY + at_y(j)}
                pl.semaphore_signal(barrier, inc=1, device_id=peer, device_id_type=MESH)
    for o in range(1, ND):
        peer = {"dp": lax.rem(d + o, ND)}
        pl.semaphore_signal(barrier, inc=1, device_id=peer, device_id_type=MESH)
    pl.semaphore_wait(barrier, NC - 1 + ND - 1)

    k1 = [
        remote(k_ref.at[:, cols(at_x(o), HD)], place(kf, x, y), K1 + o, context=at_x(o) * NY + y)
        for o in range(1, NX)
    ]
    qc, gc = {}, {}
    for o in (1, 3, 2):
        there = at_x(o) * NY + y
        qc[o] = remote(q_ref.at[:, cols(at_x(o), GW)], qb.at[x], Q + o, context=there)
        gc[o] = remote(g_ref.at[:, cols(at_x(o), GW)], gb.at[x], G + o, context=there)

    def gather_y(ref, sem):
        copies = []
        for o in range(1, NY):
            for i in range(NX):
                copies.append(
                    remote(place(ref, i, y), place(ref, i, y), sem[o] + i, context=x * NY + at_y(o))
                )
        return copies

    own[0].wait()
    for copy in k1:
        copy.wait_recv()
    k2 = gather_y(kf, {o: K2S + 4 * (o - 1) for o in range(1, NY)})

    load_x.wait()
    total = jnp.zeros((ROWS, KV), F32)
    for i in range(WCH):
        load_w[i].wait()
        part = xv[:, i * (D // WCH) : (i + 1) * (D // WCH)]
        total += jnp.dot(part, wv[i], preferred_element_type=F32)
    vown[...] = total.astype(BF)
    v_own = near(vown.at[:, cols(x, HD)], place(vf, x, y), LV)
    v1 = [
        remote(vown.at[:, cols(at_x(o), HD)], place(vf, x, y), V1 + o, context=at_x(o) * NY + y)
        for o in range(1, NX)
    ]
    v_own.wait()
    for copy in v1:
        copy.wait_recv()
    v2 = gather_y(vf, {o: V2S + 4 * (o - 1) for o in range(1, NY)})

    xc = {}
    for i in range(NX):
        for j in range(NY):
            if i or j:
                there = at_x(i) * NY + at_y(j)
                dst = xg.at[y, cols(x, ROWS), :]
                xc[i, j] = remote(x_ref.at[:, cols(there, DB)], dst, XT + NY * i + j, context=there)

    dk[...] = jnp.zeros_like(dk)
    dv[...] = jnp.zeros_like(dv)
    for copy in k2 + v2:
        copy.wait_recv()
    for o in (0, 1, 3, 2):
        if o:
            qc[o].wait_recv()
            gc[o].wait_recv()
        else:
            own[1].wait()
            own[2].wait()
        k = lax.rem(x + NX - o, NX)
        attend(k, y, length, qb, gb, kf, vf, dk, dv, qs, gs, qt, gt, p_s, d_s, m_s)

    def split_y(ref, out, got, sem, scale):
        for yy in range(NY):
            for j in range(NX):
                block = ref[(j * NY + yy) * ROWS : (j * NY + yy + 1) * ROWS, :]
                out[yy, j] = (block * scale).astype(BF) if scale else block.astype(BF)
        return [
            remote(out.at[at_y(o)], got.at[o - 1], sem + o, context=x * NY + at_y(o))
            for o in range(1, NY)
        ]

    def summed(ref, got, j, scale):
        block = ref[cols(j * NY + y, ROWS), :]
        if scale:
            block = block * scale
        for o in range(1, NY):
            block = block + got[o - 1, j].astype(F32)
        return block

    rv = split_y(dv, dvs, dvr, RV, None)
    rk = split_y(dk, dks, dkr, RK, SCALE)
    for copy in rv:
        copy.wait_recv()
    for j in range(NX):
        dvt[y, cols(x, HD), j * ROWS : (j + 1) * ROWS] = summed(dv, dvr, j, None).T.astype(BF)
    ag = {}
    for i in range(NX):
        for j in range(NY):
            if i or j:
                part = dvt.at[y, cols(x, HD), :]
                there = at_x(i) * NY + at_y(j)
                ag[i, j] = remote(part, part, AG + NY * i + j, context=there)

    for copy in rk:
        copy.wait_recv()
    for j in range(NX):
        kout[j] = summed(dk, dkr, j, SCALE).astype(BF)
    kin[x] = kout[x]
    ko = [
        remote(kout.at[at_x(o)], kin.at[x], KO + o, context=at_x(o) * NY + y) for o in range(1, NX)
    ]

    own[3].wait()
    for j in range(NY):
        for i in range(NX):
            if i or j:
                xc[i, j].wait_recv()
                ag[i, j].wait_recv()
        yy = lax.rem(y + NY - j, NY)
        part = jnp.dot(dvt[yy], xg[yy], preferred_element_type=F32)
        acc[...] = part if j == 0 else acc[...] + part
    for i in range(ND):
        gsend[i] = acc[i * CB : (i + 1) * CB, :].astype(BF)
    gr[d] = gsend[d]
    gx = [
        remote(gsend.at[lax.rem(d + o, ND)], gr.at[d], GR + o, dp=lax.rem(d + o, ND))
        for o in range(1, ND)
    ]

    squares = jnp.sum(jnp.sum(acc[...] * acc[...], axis=0, keepdims=True), axis=1, keepdims=True)
    nsend[...] = jnp.broadcast_to(squares, (8, 128))
    nx = []
    for i in range(NX):
        for j in range(NY):
            if i or j:
                slot = NY * i + j
                there = at_x(i) * NY + at_y(j)
                nx.append(remote(nsend, nr.at[c], NM + slot, context=there))
    nr[c] = nsend[...]
    for copy in nx:
        copy.wait_recv()
    squares = nr[0]
    for i in range(1, NC):
        squares = squares + nr[i]
    norm = jnp.sqrt(squares)
    nm_ref[...] = norm
    fsend[...] = CLIP / (norm + 0.01)
    fx = [
        remote(fsend, fr.at[d], FC + o, dp=lax.rem(d + o, ND)) for o in range(1, ND)
    ]
    fr[d] = fsend[...]

    for copy in ko:
        copy.wait_recv()
    for i in range(NX):
        kg_ref[:, i * HD : (i + 1) * HD] = kin[i]

    for copy in fx + gx:
        copy.wait_recv()
    clipped = fr[0][0:1, 0:1] * gr[0].astype(F32)
    for i in range(1, ND):
        clipped = clipped + fr[i][0:1, 0:1] * gr[i].astype(F32)
    clipped = jnp.concatenate([clipped, jnp.zeros((128 - CB, DB), F32)], axis=0)
    cs_ref[...] = clipped.T[:, :CB]

    for copy in sent:
        copy.wait_send()


def body(layer_input, value_weight, queries, key_states, out_grads, lengths):
    vm = pltpu.VMEM
    anywhere = pl.BlockSpec(memory_space=pl.ANY)
    inside = pl.BlockSpec(memory_space=pltpu.VMEM)
    clipped, norm, key_grads = pl.pallas_call(
        kernel,
        out_shape=(
            jax.ShapeDtypeStruct((DB, CB), F32),
            jax.ShapeDtypeStruct((8, 128), F32),
            jax.ShapeDtypeStruct((ROWS, KV), BF),
        ),
        in_specs=[pl.BlockSpec(memory_space=pltpu.SMEM)] + [anywhere] * 5,
        out_specs=(inside, inside, inside),
        scratch_shapes=[
            vm((ROWS, D), BF),
            vm((WCH, D // WCH, KV), BF),
            vm((ROWS, KV), BF),
            vm((NX, ROWS, GW), BF),
            vm((NX, ROWS, GW), BF),
            vm((SEQ, HD), BF),
            vm((SEQ, HD), BF),
            vm((NY, CK, DB), BF),
            vm((SEQ, HD), F32),
            vm((SEQ, HD), F32),
            vm((GW, HD), BF),
            vm((GW, HD), BF),
            vm((HD, GW), BF),
            vm((HD, GW), BF),
            vm((SEQ, GW), F32),
            vm((SEQ, GW), F32),
            vm((SEQ // KS, 8, GW), F32),
            vm((NY, NX, ROWS, HD), BF),
            vm((NY, NX, ROWS, HD), BF),
            vm((NY - 1, NX, ROWS, HD), BF),
            vm((NY - 1, NX, ROWS, HD), BF),
            vm((NX, ROWS, HD), BF),
            vm((NX, ROWS, HD), BF),
            vm((NY, KV, CK), BF),
            vm((KV, DB), F32),
            vm((ND, CB, DB), BF),
            vm((ND, CB, DB), BF),
            vm((8, 128), F32),
            vm((NC, 8, 128), F32),
            vm((8, 128), F32),
            vm((ND, 8, 128), F32),
            pltpu.SemaphoreType.DMA((NSEM,)),
            pltpu.SemaphoreType.DMA((NSEM,)),
            pltpu.SemaphoreType.DMA((LW + WCH,)),
        ],
        compiler_params=pltpu.CompilerParams(
            collective_id=0, has_side_effects=True, vmem_limit_bytes=56 * 2**20
        ),
    )(lengths, layer_input[0], value_weight, queries[0], key_states[0], out_grads[0])
    return clipped, norm[0, 0:1], key_grads[None]


def solution(mesh):
    placed = (
        P("dp", "context", None),
        P(),
        P("dp", "context", None),
        P("dp", "context", None),
        P("dp", "context", None),
        P("dp"),
    )
    return jax.shard_map(
        body,
        mesh=mesh,
        in_specs=placed,
        out_specs=(P("context", "dp"), P("dp"), P("dp", "context", None)),
        check_vma=False,
    )
```

time: 476 us -> 149 us (0.31)
  waiting for transfers between devices: 181 us -> 0 us
  Pallas kernels: 0 us -> 143 us
  matrix products: 96 us -> 0 us
  blocking collectives: 61.9 us -> 0 us
  other arithmetic: 58.1 us -> 0 us
  local copies, waits for them, and re-layouts: 33 us -> 4.44 us
  starting transfers between devices: 25.7 us -> 0 us
  between operations: 16.1 us -> 1.29 us
    reduce_scatter x2 -> x0, waiting for transfers between devices: 145 us -> none  [the longest x1 99.9 us: body(): lax.psum_scatter(lax.dot_general(input_part, value_low, contract_rows, pr...]
    pallas_call x0 -> x1, Pallas kernels: none -> 143 us  [body(): pl.pallas_call(kernel, out_shape=(jax.ShapeDtypeStruct((DB, CB), F32), ja...]
    dot_general x14 -> x0, matrix products: 66.4 us -> none  [the longest x4 30.5 us: attend_block(): jnp.einsum('hij,ihd->jhd', grad_scores, query_block, preferred_element_ty...]
    all_to_all x5 -> x0, waiting for transfers between devices: 35.4 us -> none  [the longest x1 14.2 us: body(): lax.all_to_all(grad_split, 'context', split_axis=1, concat_axis=0, tiled=...]
    psum x1 -> x0, blocking collectives: 32 us -> none  [body(): total_squares = lax.psum(partial_value, 'context')]
    all_to_all x1 -> x0, blocking collectives: 29.9 us -> none  [body(): lax.all_to_all(value_grad, 'context', split_axis=0, concat_axis=1, tiled=...]
    convert_element_type x6 -> x0, other arithmetic: 29.7 us -> none  [the longest x4 26.4 us: attend_block(): probs_low = weights.astype(jnp.bfloat16)]
    sub x4 -> x0, matrix products: 29.6 us -> none  [attend_block(): weights = jnp.exp(scores - row_peak)]
  transfers between devices with their start and end apart: 7 -> 0, of which waited for: 6 -> 0; matrix products, arithmetic and copies ran while one was open for 7% -> 0% of each run, Pallas kernels for 0% -> 0%
where the time goes in v1:
time: 149 us
  Pallas kernels  143 us (96%)
  local copies, waits for them, and re-layouts  4.44 us (3%)
    pallas_call x1, Pallas kernels, body(): pl.pallas_call(kernel, out_shape=(jax.ShapeDtypeStruct((DB, CB), F32), ja...  143 us
    unnamed x2, local copies, waits for them, and re-layouts  3.25 us

profile of v1, /device:TPU:1, one launch (start us, length us, event | category | flops | bytes accessed | tf_op | source)
XLA Modules:
  0.0 148.6 jit_solution(3357651602582338123)
XLA Ops:
  1.3 142.9 %shard_map.85 = (f32[512,32]{1,0:T(8,128)}, f32[8,128]{1,0:T(8,128)}, bf16[128,512]{1,0:T(8,128)(2,1)}) custom-call(s32[1]{0:T(128)S(6)} %copy.11.len_ref, bf16[128,8192]{1,0:T(8,128)(2,1)} %bitcast.6, bf16[8192,512]{1,0:T(8,128)(2,1)} %w_ref.1, bf16[128,4096]{1,0:T(8,128)(2,1)} %bitcast.7, bf16[128,512]{1,0:T(8,128)(2,1)} %bitcast.9, bf16[128,4096]{1,0:T(8,128)(2,1)} %bitcast.8), custom_call_target="tpu_custom_call" | custom-call | tf_op jit(solution)/shard_map/pallas_call | solution.py:317
  144.1 1.2 slice.3
  145.3 1.7 %copy.9 = f32[512,32]{0,1:T(8,128)} copy(f32[512,32]{1,0:T(8,128)} %get-tuple-element.9) | data formatting | bytes 131072
  147.0 1.6 %copy.12 = bf16[1,128,512]{2,1,0:T(8,128)(2,1)} copy(bf16[1,128,512]{2,1,0:T(8,128)(2,1)} %bitcast.10) | data formatting | bytes 262144

commit v2 on v1

--- a/solution.py
+++ b/solution.py
@@ -24,7 +24,7 @@
 GW = GH * HD
 SEQ = NC * ROWS
 CK = NY * ROWS
-KS = 256
+KS = 512
 STEPS = CK // KS
 DB = D // NC
 CB = KV // ND
@@ -33,10 +33,10 @@
 C2 = SCALE * math.log2(math.e)
 CLIP = math.sqrt(D * KV)
 
-K1, Q, G, K2, V1, V2, RV, RK, KO = range(0, 36, 4)
-XT, AG, NM, GR, FC = range(36, 36 + 80, 16)
-K2S, V2S, NSEM = 116, 128, 140
-LX, LQ, LG, LK, LV, LXG, LW = 0, 1, 2, 3, 4, 5, 6
+K1, Q, G, V1, RV, RK, KO, AX, AY, NA, NB = range(0, 44, 4)
+K2, V2, XY, XX, AXF, AYF, GR, FC = range(44, 44 + 128, 16)
+NSEM = 172
+LX, LQ, LG, LK, LV, LXG, LW = 0, 1, 2, 3, 4, 5, 9
 
 
 def attend(k, y, length, qb, gb, kf, vf, dk, dv, qs, gs, qt, gt, p_s, d_s, m_s):
@@ -93,7 +93,7 @@
 def kernel(
     len_ref, x_ref, w_ref, q_ref, k_ref, g_ref,
     cs_ref, nm_ref, kg_ref,
-    xv, wv, vown, qb, gb, kf, vf, xg, dk, dv, qs, gs, qt, gt, p_s, d_s, m_s,
+    xv, wv, vown, qb, gb, kf, vf, xg, xs, dk, dv, qs, gs, qt, gt, p_s, d_s, m_s,
     dvs, dks, dvr, dkr, kout, kin, dvt, acc, gsend, gr, nsend, nr, fsend, fr,
     send, recv, local,
 ):
@@ -135,43 +135,59 @@
         near(k_ref.at[:, cols(x, HD)], place(kf, x, y), LK),
         near(q_ref.at[:, cols(x, GW)], qb.at[x], LQ),
         near(g_ref.at[:, cols(x, GW)], gb.at[x], LG),
-        near(x_ref.at[:, cols(c, DB)], xg.at[y, cols(x, ROWS), :], LXG),
-    ]
+    ]
+
+    def staged(i, yi):
+        return xs.at[i - 1, yi] if i else xg.at[yi, x]
+
+    for i in range(NX):
+        own.append(near(x_ref.at[:, cols(at_x(i) * NY + y, DB)], staged(i, y), LXG + i))
+
+    def on_x(o):
+        return {"context": at_x(o) * NY + y}
+
+    def on_y(o):
+        return {"context": x * NY + at_y(o)}
+
+    def on_dp(o):
+        return {"dp": lax.rem(d + o, ND)}
 
     barrier = pltpu.get_barrier_semaphore()
-    for i in range(NX):
-        for j in range(NY):
-            if i or j:
-                peer = {"context": at_x(i) * NY + at_y(j)}
-                pl.semaphore_signal(barrier, inc=1, device_id=peer, device_id_type=MESH)
-    for o in range(1, ND):
-        peer = {"dp": lax.rem(d + o, ND)}
+    peers = [on_x(o) for o in range(1, NX)] + [on_y(o) for o in range(1, NY)]
+    peers += [on_dp(o) for o in range(1, ND)]
+    for peer in peers:
         pl.semaphore_signal(barrier, inc=1, device_id=peer, device_id_type=MESH)
-    pl.semaphore_wait(barrier, NC - 1 + ND - 1)
+    pl.semaphore_wait(barrier, len(peers))
 
     k1 = [
-        remote(k_ref.at[:, cols(at_x(o), HD)], place(kf, x, y), K1 + o, context=at_x(o) * NY + y)
+        remote(k_ref.at[:, cols(at_x(o), HD)], place(kf, x, y), K1 + o, **on_x(o))
         for o in range(1, NX)
     ]
     qc, gc = {}, {}
-    for o in (1, 3, 2):
-        there = at_x(o) * NY + y
-        qc[o] = remote(q_ref.at[:, cols(at_x(o), GW)], qb.at[x], Q + o, context=there)
-        gc[o] = remote(g_ref.at[:, cols(at_x(o), GW)], gb.at[x], G + o, context=there)
+
+
+    def queries_x(o):
+        qc[o] = remote(q_ref.at[:, cols(at_x(o), GW)], qb.at[x], Q + o, **on_x(o))
+
+    def grads_x(o):
+        gc[o] = remote(g_ref.at[:, cols(at_x(o), GW)], gb.at[x], G + o, **on_x(o))
+
+    queries_x(1)
+    queries_x(3)
 
     def gather_y(ref, sem):
         copies = []
         for o in range(1, NY):
             for i in range(NX):
                 copies.append(
-                    remote(place(ref, i, y), place(ref, i, y), sem[o] + i, context=x * NY + at_y(o))
+                    remote(place(ref, i, y), place(ref, i, y), sem + NX * o + i, **on_y(o))
                 )
         return copies
 
     own[0].wait()
     for copy in k1:
         copy.wait_recv()
-    k2 = gather_y(kf, {o: K2S + 4 * (o - 1) for o in range(1, NY)})
+    k2 = gather_y(kf, K2)
 
     load_x.wait()
     total = jnp.zeros((ROWS, KV), F32)
@@ -182,26 +198,42 @@
     vown[...] = total.astype(BF)
     v_own = near(vown.at[:, cols(x, HD)], place(vf, x, y), LV)
     v1 = [
-        remote(vown.at[:, cols(at_x(o), HD)], place(vf, x, y), V1 + o, context=at_x(o) * NY + y)
+        remote(vown.at[:, cols(at_x(o), HD)], place(vf, x, y), V1 + o, **on_x(o))
         for o in range(1, NX)
     ]
+    grads_x(1)
+    grads_x(3)
+    queries_x(2)
+    grads_x(2)
     v_own.wait()
     for copy in v1:
         copy.wait_recv()
-    v2 = gather_y(vf, {o: V2S + 4 * (o - 1) for o in range(1, NY)})
-
-    xc = {}
-    for i in range(NX):
-        for j in range(NY):
-            if i or j:
-                there = at_x(i) * NY + at_y(j)
-                dst = xg.at[y, cols(x, ROWS), :]
-                xc[i, j] = remote(x_ref.at[:, cols(there, DB)], dst, XT + NY * i + j, context=there)
-
+    v2 = gather_y(vf, V2)
+
+    xy, xx = {}, {}
+
+    def input_y(i):
+        for o in range(1, NY):
+            there = at_x(i) * NY + at_y(o)
+            xy[i, o] = remote(
+                x_ref.at[:, cols(there, DB)], staged(i, y), XY + NX * o + i, **on_y(o)
+            )
+
+    def input_x(i):
+        own[3 + i].wait()
+        for o in range(1, NY):
+            xy[i, o].wait_recv()
+        if i:
+            xx[i] = remote(xs.at[i - 1], xg.at[:, x], XX + i, **on_x(i))
+
+    input_y(1)
+    input_y(3)
     dk[...] = jnp.zeros_like(dk)
     dv[...] = jnp.zeros_like(dv)
     for copy in k2 + v2:
         copy.wait_recv()
+    input_y(2)
+    input_y(0)
     for o in (0, 1, 3, 2):
         if o:
             qc[o].wait_recv()
@@ -211,6 +243,11 @@
             own[2].wait()
         k = lax.rem(x + NX - o, NX)
         attend(k, y, length, qb, gb, kf, vf, dk, dv, qs, gs, qt, gt, p_s, d_s, m_s)
+        if o == 1:
+            input_x(1)
+            input_x(3)
+        elif o == 3:
+            input_x(2)
 
     def split_y(ref, out, got, sem, scale):
         for yy in range(NY):
@@ -218,7 +255,7 @@
                 block = ref[(j * NY + yy) * ROWS : (j * NY + yy + 1) * ROWS, :]
                 out[yy, j] = (block * scale).astype(BF) if scale else block.astype(BF)
         return [
-            remote(out.at[at_y(o)], got.at[o - 1], sem + o, context=x * NY + at_y(o))
+            remote(out.at[at_y(o)], got.at[o - 1], sem + o, **on_y(o))
             for o in range(1, NY)
         ]
 
@@ -231,68 +268,72 @@
         return block
 
     rv = split_y(dv, dvs, dvr, RV, None)
-    rk = split_y(dk, dks, dkr, RK, SCALE)
     for copy in rv:
         copy.wait_recv()
     for j in range(NX):
         dvt[y, cols(x, HD), j * ROWS : (j + 1) * ROWS] = summed(dv, dvr, j, None).T.astype(BF)
-    ag = {}
-    for i in range(NX):
-        for j in range(NY):
-            if i or j:
-                part = dvt.at[y, cols(x, HD), :]
-                there = at_x(i) * NY + at_y(j)
-                ag[i, j] = remote(part, part, AG + NY * i + j, context=there)
-
-    for copy in rk:
-        copy.wait_recv()
-    for j in range(NX):
-        kout[j] = summed(dk, dkr, j, SCALE).astype(BF)
-    kin[x] = kout[x]
-    ko = [
-        remote(kout.at[at_x(o)], kin.at[x], KO + o, context=at_x(o) * NY + y) for o in range(1, NX)
-    ]
-
-    own[3].wait()
+    half = CK // 2
+    part = dvt.at[y, cols(x, HD), :]
+    ax, ay, axf, ayf = {}, {}, {}, {}
+    for o in (1, 3, 2):
+        ax[o] = remote(part, part, AX + o, **on_x(o))
+        ay[o] = remote(part, part, AY + o, **on_y(o))
+    for o in (1, 3, 2):
+        ax[o].wait_recv()
+        part = dvt.at[y, cols(lax.rem(x + NX - o, NX), HD), half:]
+        for j in (1, 3, 2):
+            ayf[o, j] = remote(part, part, AYF + NY * o + j, **on_y(j))
+        ay[o].wait_recv()
+        part = dvt.at[lax.rem(y + NY - o, NY), cols(x, HD), :half]
+        for i in (1, 3, 2):
+            axf[i, o] = remote(part, part, AXF + NY * i + o, **on_x(i))
+    rk = split_y(dk, dks, dkr, RK, SCALE)
+
+    input_x(0)
+    for i in range(1, NX):
+        xx[i].wait_recv()
     for j in range(NY):
-        for i in range(NX):
-            if i or j:
-                xc[i, j].wait_recv()
-                ag[i, j].wait_recv()
+        for i in range(1, NX):
+            if j:
+                axf[i, j].wait_recv()
+                ayf[i, j].wait_recv()
         yy = lax.rem(y + NY - j, NY)
-        part = jnp.dot(dvt[yy], xg[yy], preferred_element_type=F32)
+        part = jnp.dot(dvt[yy], xg[yy].reshape(CK, DB), preferred_element_type=F32)
         acc[...] = part if j == 0 else acc[...] + part
     for i in range(ND):
         gsend[i] = acc[i * CB : (i + 1) * CB, :].astype(BF)
     gr[d] = gsend[d]
     gx = [
-        remote(gsend.at[lax.rem(d + o, ND)], gr.at[d], GR + o, dp=lax.rem(d + o, ND))
+        remote(gsend.at[lax.rem(d + o, ND)], gr.at[d], GR + o, **on_dp(o))
         for o in range(1, ND)
     ]
 
     squares = jnp.sum(jnp.sum(acc[...] * acc[...], axis=0, keepdims=True), axis=1, keepdims=True)
-    nsend[...] = jnp.broadcast_to(squares, (8, 128))
-    nx = []
-    for i in range(NX):
-        for j in range(NY):
-            if i or j:
-                slot = NY * i + j
-                there = at_x(i) * NY + at_y(j)
-                nx.append(remote(nsend, nr.at[c], NM + slot, context=there))
-    nr[c] = nsend[...]
-    for copy in nx:
-        copy.wait_recv()
-    squares = nr[0]
-    for i in range(1, NC):
-        squares = squares + nr[i]
+    squares = jnp.broadcast_to(squares, (8, 128))
+    for step, (on, sem) in enumerate(((on_x, NA), (on_y, NB))):
+        mine = y if step else x
+        nsend[step] = squares
+        copies = [remote(nsend.at[step], nr.at[step, mine], sem + o, **on(o)) for o in range(1, NX)]
+        nr[step, mine] = squares
+        for copy in copies:
+            copy.wait_recv()
+        squares = (nr[step, 0] + nr[step, 1]) + (nr[step, 2] + nr[step, 3])
     norm = jnp.sqrt(squares)
     nm_ref[...] = norm
     fsend[...] = CLIP / (norm + 0.01)
     fx = [
-        remote(fsend, fr.at[d], FC + o, dp=lax.rem(d + o, ND)) for o in range(1, ND)
+        remote(fsend, fr.at[d], FC + o, **on_dp(o)) for o in range(1, ND)
     ]
     fr[d] = fsend[...]
 
+    for copy in rk:
+        copy.wait_recv()
+    for j in range(NX):
+        kout[j] = summed(dk, dkr, j, SCALE).astype(BF)
+    kin[x] = kout[x]
+    ko = [
+        remote(kout.at[at_x(o)], kin.at[x], KO + o, **on_x(o)) for o in range(1, NX)
+    ]
     for copy in ko:
         copy.wait_recv()
     for i in range(NX):
@@ -331,7 +372,8 @@
             vm((NX, ROWS, GW), BF),
             vm((SEQ, HD), BF),
             vm((SEQ, HD), BF),
-            vm((NY, CK, DB), BF),
+            vm((NY, NX, ROWS, DB), BF),
+            vm((NX - 1, NY, ROWS, DB), BF),
             vm((SEQ, HD), F32),
             vm((SEQ, HD), F32),
             vm((GW, HD), BF),
@@ -351,8 +393,8 @@
             vm((KV, DB), F32),
             vm((ND, CB, DB), BF),
             vm((ND, CB, DB), BF),
-            vm((8, 128), F32),
-            vm((NC, 8, 128), F32),
+            vm((2, 8, 128), F32),
+            vm((2, NX, 8, 128), F32),
             vm((8, 128), F32),
             vm((ND, 8, 128), F32),
             pltpu.SemaphoreType.DMA((NSEM,)),

time: 149 us -> 102 us (0.68)
  Pallas kernels: 143 us -> 95.8 us
    pallas_call x1, Pallas kernels: 143 us -> 95.8 us  [body(): pl.pallas_call(kernel, out_shape=(jax.ShapeDtypeStruct((DB, CB), F32), ja...]
where the time goes in v2:
time: 102 us
  Pallas kernels  95.8 us (94%)
  local copies, waits for them, and re-layouts  4.44 us (4%)
  between operations  1.29 us (1%)
    pallas_call x1, Pallas kernels, body(): pl.pallas_call(kernel, out_shape=(jax.ShapeDtypeStruct((DB, CB), F32), ja...  95.8 us
    unnamed x2, local copies, waits for them, and re-layouts  3.25 us

profile of v2, /device:TPU:1, one launch (start us, length us, event | category | flops | bytes accessed | tf_op | source)
XLA Modules:
  0.0 101.5 jit_solution(15299464400918823976)
XLA Ops:
  1.3 95.8 %shard_map.85 = (f32[512,32]{1,0:T(8,128)}, f32[8,128]{1,0:T(8,128)}, bf16[128,512]{1,0:T(8,128)(2,1)}) custom-call(s32[1]{0:T(128)S(6)} %copy.11.len_ref, bf16[128,8192]{1,0:T(8,128)(2,1)} %bitcast.6, bf16[8192,512]{1,0:T(8,128)(2,1)} %w_ref.1, bf16[128,4096]{1,0:T(8,128)(2,1)} %bitcast.7, bf16[128,512]{1,0:T(8,128)(2,1)} %bitcast.9, bf16[128,4096]{1,0:T(8,128)(2,1)} %bitcast.8), custom_call_target="tpu_custom_call" | custom-call | tf_op jit(solution)/shard_map/pallas_call | solution.py:358
  97.1 1.2 %slice.3 = f32[1,1]{1,0:T(1,128)} slice(f32[8,128]{1,0:T(8,128)} %get-tuple-element.7), slice={[0:1], [0:1]} | slice | bytes 8 | tf_op jit(solution)/shard_map/slice | solution.py:408
  98.3 1.7 %copy.9 = f32[512,32]{0,1:T(8,128)} copy(f32[512,32]{1,0:T(8,128)} %get-tuple-element.9) | data formatting | bytes 131072
  99.9 1.6 %copy.12 = bf16[1,128,512]{2,1,0:T(8,128)(2,1)} copy(bf16[1,128,512]{2,1,0:T(8,128)(2,1)} %bitcast.10) | data formatting | bytes 262144

commit v3 on v2

--- a/solution.py
+++ b/solution.py
@@ -27,19 +27,19 @@
 KS = 512
 STEPS = CK // KS
 DB = D // NC
+DH = DB // 2
 CB = KV // ND
 WCH = 8
 SCALE = HD ** (-0.5)
 C2 = SCALE * math.log2(math.e)
 CLIP = math.sqrt(D * KV)
 
-K1, Q, G, V1, RV, RK, KO, AX, AY, NA, NB = range(0, 44, 4)
-K2, V2, XY, XX, AXF, AYF, GR, FC = range(44, 44 + 128, 16)
-NSEM = 172
-LX, LQ, LG, LK, LV, LXG, LW = 0, 1, 2, 3, 4, 5, 9
-
-
-def attend(k, y, length, qb, gb, kf, vf, dk, dv, qs, gs, qt, gt, p_s, d_s, m_s):
+K1, Q, G, V1, RK, KO, AX, AY = range(0, 32, 4)
+K2, V2, XY, XX, AXF, AYF, GR, FC, RV, NM = range(32, 32 + 10 * 32, 32)
+NSEM = 352
+LX, LQ, LG, LK, LV, LXG, LW = 0, 1, 2, 3, 4, 5, 13
+
+def attend(k, y, length, qb, gb, kf, vf, dk, dv, qs, gs, qt, gt, p_s, d_s, m_s, done):
     q_pos = CK * k + ROWS * y + lax.broadcasted_iota(jnp.int32, (ROWS, HD), 0)
     keep = q_pos < length
     for h in range(GH):
@@ -85,10 +85,11 @@
         ds = p * (d_s[rows, :] - off)
         dv[rows, :] += jnp.dot(p.astype(BF), gs[...], preferred_element_type=F32)
         dk[rows, :] += jnp.dot(ds.astype(BF), qs[...], preferred_element_type=F32)
+        if done:
+            done(j)
         return 0
 
     lax.fori_loop(0, (k + 1) * STEPS, sweep_b, 0)
-
 
 def kernel(
     len_ref, x_ref, w_ref, q_ref, k_ref, g_ref,
@@ -137,11 +138,16 @@
         near(g_ref.at[:, cols(x, GW)], gb.at[x], LG),
     ]
 
-    def staged(i, yi):
-        return xs.at[i - 1, yi] if i else xg.at[yi, x]
-
-    for i in range(NX):
-        own.append(near(x_ref.at[:, cols(at_x(i) * NY + y, DB)], staged(i, y), LXG + i))
+    def staged(h, i, yi):
+        return xs.at[h, i - 1, yi] if i else xg.at[h, yi, x]
+
+    def input_cols(h, there):
+        return x_ref.at[:, pl.ds(pl.multiple_of(there * DB + h * DH, DH), DH)]
+
+    for h in range(2):
+        for i in range(NX):
+            src = input_cols(h, at_x(i) * NY + y)
+            own.append(near(src, staged(h, i, y), LXG + NX * h + i))
 
     def on_x(o):
         return {"context": at_x(o) * NY + y}
@@ -152,28 +158,47 @@
     def on_dp(o):
         return {"dp": lax.rem(d + o, ND)}
 
+    def on_xy(i, j):
+        return {"context": at_x(i) * NY + at_y(j)}
+
     barrier = pltpu.get_barrier_semaphore()
-    peers = [on_x(o) for o in range(1, NX)] + [on_y(o) for o in range(1, NY)]
-    peers += [on_dp(o) for o in range(1, ND)]
+    others = [(i, j) for i in range(NX) for j in range(NY) if i or j]
+    peers = [on_xy(i, j) for i, j in others] + [on_dp(o) for o in range(1, ND)]
     for peer in peers:
         pl.semaphore_signal(barrier, inc=1, device_id=peer, device_id_type=MESH)
+
+    dk[...] = jnp.zeros_like(dk)
+    dv[...] = jnp.zeros_like(dv)
+    load_x.wait()
+    total = jnp.zeros((ROWS, KV), F32)
+    for i in range(WCH):
+        load_w[i].wait()
+        part = xv[:, i * (D // WCH) : (i + 1) * (D // WCH)]
+        total += jnp.dot(part, wv[i], preferred_element_type=F32)
+    vown[...] = total.astype(BF)
+    v_own = near(vown.at[:, cols(x, HD)], place(vf, x, y), LV)
+
     pl.semaphore_wait(barrier, len(peers))
 
+    v1 = [
+        remote(vown.at[:, cols(at_x(o), HD)], place(vf, x, y), V1 + o, **on_x(o))
+        for o in range(1, NX)
+    ]
     k1 = [
         remote(k_ref.at[:, cols(at_x(o), HD)], place(kf, x, y), K1 + o, **on_x(o))
         for o in range(1, NX)
     ]
     qc, gc = {}, {}
 
-
     def queries_x(o):
         qc[o] = remote(q_ref.at[:, cols(at_x(o), GW)], qb.at[x], Q + o, **on_x(o))
 
     def grads_x(o):
         gc[o] = remote(g_ref.at[:, cols(at_x(o), GW)], gb.at[x], G + o, **on_x(o))
 
-    queries_x(1)
-    queries_x(3)
+    for o in (1, 3, 2):
+        queries_x(o)
+        grads_x(o)
 
     def gather_y(ref, sem):
         copies = []
@@ -189,22 +214,6 @@
         copy.wait_recv()
     k2 = gather_y(kf, K2)
 
-    load_x.wait()
-    total = jnp.zeros((ROWS, KV), F32)
-    for i in range(WCH):
-        load_w[i].wait()
-        part = xv[:, i * (D // WCH) : (i + 1) * (D // WCH)]
-        total += jnp.dot(part, wv[i], preferred_element_type=F32)
-    vown[...] = total.astype(BF)
-    v_own = near(vown.at[:, cols(x, HD)], place(vf, x, y), LV)
-    v1 = [
-        remote(vown.at[:, cols(at_x(o), HD)], place(vf, x, y), V1 + o, **on_x(o))
-        for o in range(1, NX)
-    ]
-    grads_x(1)
-    grads_x(3)
-    queries_x(2)
-    grads_x(2)
     v_own.wait()
     for copy in v1:
         copy.wait_recv()
@@ -212,28 +221,39 @@
 
     xy, xx = {}, {}
 
-    def input_y(i):
+    def input_y(h, i):
         for o in range(1, NY):
-            there = at_x(i) * NY + at_y(o)
-            xy[i, o] = remote(
-                x_ref.at[:, cols(there, DB)], staged(i, y), XY + NX * o + i, **on_y(o)
-            )
-
-    def input_x(i):
-        own[3 + i].wait()
+            src = input_cols(h, at_x(i) * NY + at_y(o))
+            sem = XY + NC * h + NX * o + i
+            xy[h, i, o] = remote(src, staged(h, i, y), sem, **on_y(o))
+
+    def input_x(h, i):
+        own[3 + NX * h + i].wait()
         for o in range(1, NY):
-            xy[i, o].wait_recv()
+            xy[h, i, o].wait_recv()
         if i:
-            xx[i] = remote(xs.at[i - 1], xg.at[:, x], XX + i, **on_x(i))
-
-    input_y(1)
-    input_y(3)
-    dk[...] = jnp.zeros_like(dk)
-    dv[...] = jnp.zeros_like(dv)
+            xx[h, i] = remote(xs.at[h, i - 1], xg.at[h, :, x], XX + NX * h + i, **on_x(i))
+
+    for i in (1, 3, 2, 0):
+        input_y(0, i)
     for copy in k2 + v2:
         copy.wait_recv()
-    input_y(2)
-    input_y(0)
+    for i in (1, 3, 2, 0):
+        input_y(1, i)
+    def sum_copy(o, j):
+        sem = RV + NX * o + j
+        return pltpu.make_async_remote_copy(
+            src_ref=dvs.at[at_y(o), j], dst_ref=dvr.at[o - 1, j], send_sem=send.at[sem],
+            recv_sem=recv.at[sem], device_id=on_y(o), device_id_type=MESH,
+        )
+
+    def sum_start(j):
+        for yy in range(NY):
+            dvs[yy, j] = dv[cols(j * NY + yy, ROWS), :].astype(BF)
+        for o in range(1, NY):
+            sum_copy(o, j).start()
+        return 0
+
     for o in (0, 1, 3, 2):
         if o:
             qc[o].wait_recv()
@@ -242,12 +262,16 @@
             own[1].wait()
             own[2].wait()
         k = lax.rem(x + NX - o, NX)
-        attend(k, y, length, qb, gb, kf, vf, dk, dv, qs, gs, qt, gt, p_s, d_s, m_s)
+        done = None
+        if o == 2:
+            done = sum_start
+            lax.fori_loop(k + 1, NX, lambda j, _: sum_start(j), 0)
+        attend(k, y, length, qb, gb, kf, vf, dk, dv, qs, gs, qt, gt, p_s, d_s, m_s, done)
         if o == 1:
-            input_x(1)
-            input_x(3)
+            input_x(0, 1)
+            input_x(0, 3)
         elif o == 3:
-            input_x(2)
+            input_x(0, 2)
 
     def split_y(ref, out, got, sem, scale):
         for yy in range(NY):
@@ -267,7 +291,10 @@
             block = block + got[o - 1, j].astype(F32)
         return block
 
-    rv = split_y(dv, dvs, dvr, RV, None)
+    rv = [sum_copy(o, j) for j in range(NX) for o in range(1, NY)]
+    sent.extend(rv)
+    input_x(1, 1)
+    input_x(1, 3)
     for copy in rv:
         copy.wait_recv()
     for j in range(NX):
@@ -287,37 +314,41 @@
         part = dvt.at[lax.rem(y + NY - o, NY), cols(x, HD), :half]
         for i in (1, 3, 2):
             axf[i, o] = remote(part, part, AXF + NY * i + o, **on_x(i))
+    input_x(1, 2)
     rk = split_y(dk, dks, dkr, RK, SCALE)
 
-    input_x(0)
-    for i in range(1, NX):
-        xx[i].wait_recv()
-    for j in range(NY):
+    squares = jnp.zeros((1, 1), F32)
+    gx = []
+    for h in range(2):
+        input_x(h, 0)
         for i in range(1, NX):
-            if j:
-                axf[i, j].wait_recv()
-                ayf[i, j].wait_recv()
-        yy = lax.rem(y + NY - j, NY)
-        part = jnp.dot(dvt[yy], xg[yy].reshape(CK, DB), preferred_element_type=F32)
-        acc[...] = part if j == 0 else acc[...] + part
-    for i in range(ND):
-        gsend[i] = acc[i * CB : (i + 1) * CB, :].astype(BF)
-    gr[d] = gsend[d]
-    gx = [
-        remote(gsend.at[lax.rem(d + o, ND)], gr.at[d], GR + o, **on_dp(o))
-        for o in range(1, ND)
-    ]
-
-    squares = jnp.sum(jnp.sum(acc[...] * acc[...], axis=0, keepdims=True), axis=1, keepdims=True)
-    squares = jnp.broadcast_to(squares, (8, 128))
-    for step, (on, sem) in enumerate(((on_x, NA), (on_y, NB))):
-        mine = y if step else x
-        nsend[step] = squares
-        copies = [remote(nsend.at[step], nr.at[step, mine], sem + o, **on(o)) for o in range(1, NX)]
-        nr[step, mine] = squares
-        for copy in copies:
-            copy.wait_recv()
-        squares = (nr[step, 0] + nr[step, 1]) + (nr[step, 2] + nr[step, 3])
+            xx[h, i].wait_recv()
+        for j in (0, 1, 3, 2):
+            if h == 0:
+                for i in range(1, NX):
+                    if j:
+                        axf[i, j].wait_recv()
+                        ayf[i, j].wait_recv()
+            yy = lax.rem(y + NY - j, NY)
+            part = jnp.dot(dvt[yy], xg[h, yy].reshape(CK, DH), preferred_element_type=F32)
+            acc[...] = acc[...] + part if j else part
+        total = acc[...]
+        for i in range(ND):
+            gsend[h, i] = total[i * CB : (i + 1) * CB, :].astype(BF)
+        gr[h, d] = gsend[h, d]
+        for o in range(1, ND):
+            there = lax.rem(d + o, ND)
+            gx.append(remote(gsend.at[h, there], gr.at[h, d], GR + ND * h + o, **on_dp(o)))
+        columns = jnp.sum(total * total, axis=0, keepdims=True)
+        squares = squares + jnp.sum(columns, axis=1, keepdims=True)
+    nsend[...] = jnp.broadcast_to(squares, (8, 128))
+    nx = [remote(nsend, nr.at[c], NM + NY * i + j, **on_xy(i, j)) for i, j in others]
+    nr[c] = nsend[...]
+    for copy in nx:
+        copy.wait_recv()
+    squares = nr[0]
+    for i in range(1, NC):
+        squares = squares + nr[i]
     norm = jnp.sqrt(squares)
     nm_ref[...] = norm
     fsend[...] = CLIP / (norm + 0.01)
@@ -341,15 +372,19 @@
 
     for copy in fx + gx:
         copy.wait_recv()
-    clipped = fr[0][0:1, 0:1] * gr[0].astype(F32)
-    for i in range(1, ND):
-        clipped = clipped + fr[i][0:1, 0:1] * gr[i].astype(F32)
-    clipped = jnp.concatenate([clipped, jnp.zeros((128 - CB, DB), F32)], axis=0)
-    cs_ref[...] = clipped.T[:, :CB]
+    for h in range(2):
+        clipped = fr[0][0:1, 0:1] * gr[h, 0].astype(F32)
+        for i in range(1, ND):
+            clipped = clipped + fr[i][0:1, 0:1] * gr[h, i].astype(F32)
+        cs_ref[:, h * DH : (h + 1) * DH] = clipped
 
     for copy in sent:
         copy.wait_send()
 
+def finish(clipped_ref, norm_ref, key_ref, cs_ref, nm_ref, kg_ref):
+    cs_ref[...] = clipped_ref[...]
+    nm_ref[0] = norm_ref[0, 0]
+    kg_ref[0] = key_ref[...]
 
 def body(layer_input, value_weight, queries, key_states, out_grads, lengths):
     vm = pltpu.VMEM
@@ -358,7 +393,7 @@
     clipped, norm, key_grads = pl.pallas_call(
         kernel,
         out_shape=(
-            jax.ShapeDtypeStruct((DB, CB), F32),
+            jax.ShapeDtypeStruct((CB, DB), F32),
             jax.ShapeDtypeStruct((8, 128), F32),
             jax.ShapeDtypeStruct((ROWS, KV), BF),
         ),
@@ -372,8 +407,8 @@
             vm((NX, ROWS, GW), BF),
             vm((SEQ, HD), BF),
             vm((SEQ, HD), BF),
-            vm((NY, NX, ROWS, DB), BF),
-            vm((NX - 1, NY, ROWS, DB), BF),
+            vm((2, NY, NX, ROWS, DH), BF),
+            vm((2, NX - 1, NY, ROWS, DH), BF),
             vm((SEQ, HD), F32),
             vm((SEQ, HD), F32),
             vm((GW, HD), BF),
@@ -390,11 +425,11 @@
             vm((NX, ROWS, HD), BF),
             vm((NX, ROWS, HD), BF),
             vm((NY, KV, CK), BF),
-            vm((KV, DB), F32),
-            vm((ND, CB, DB), BF),
-            vm((ND, CB, DB), BF),
-            vm((2, 8, 128), F32),
-            vm((2, NX, 8, 128), F32),
+            vm((KV, DH), F32),
+            vm((2, ND, CB, DH), BF),
+            vm((2, ND, CB, DH), BF),
+            vm((8, 128), F32),
+            vm((NC, 8, 128), F32),
             vm((8, 128), F32),
             vm((ND, 8, 128), F32),
             pltpu.SemaphoreType.DMA((NSEM,)),
@@ -405,8 +440,17 @@
             collective_id=0, has_side_effects=True, vmem_limit_bytes=56 * 2**20
         ),
     )(lengths, layer_input[0], value_weight, queries[0], key_states[0], out_grads[0])
-    return clipped, norm[0, 0:1], key_grads[None]
-
+    clipped, norm, key_grads = pl.pallas_call(
+        finish,
+        out_shape=(
+            jax.ShapeDtypeStruct((CB, DB), F32),
+            jax.ShapeDtypeStruct((1,), F32),
+            jax.ShapeDtypeStruct((1, ROWS, KV), BF),
+        ),
+        in_specs=[inside, pl.BlockSpec(memory_space=pltpu.SMEM), inside],
+        out_specs=(inside, pl.BlockSpec(memory_space=pltpu.SMEM), inside),
+    )(clipped, norm, key_grads)
+    return clipped.T, norm, key_grads
 
 def solution(mesh):
     placed = (

time: 102 us -> 103 us (level)
  Pallas kernels: 95.8 us -> 102 us
  local copies, waits for them, and re-layouts: 4.44 us -> 0 us
    pallas_call x1 -> x2, Pallas kernels: 95.8 us -> 102 us  [the longest x1 100 us: body(): pl.pallas_call(kernel, out_shape=(jax.ShapeDtypeStruct((CB, DB), F32), ja...]
    unnamed x2 -> x0, local copies, waits for them, and re-layouts: 3.25 us -> none
    slice x1 -> x0, local copies, waits for them, and re-layouts: 1.18 us -> none  [body(): return (clipped, norm[0, 0:1], key_grads[None])]
where the time goes in v3:
time: 103 us
  Pallas kernels  102 us (99%)
  between operations  1.45 us (1%)
    pallas_call x1, Pallas kernels, body(): pl.pallas_call(kernel, out_shape=(jax.ShapeDtypeStruct((CB, DB), F32), ja...  100 us

profile of v3, /device:TPU:1, one launch (start us, length us, event | category | flops | bytes accessed | tf_op | source)
XLA Modules:
  0.0 103.3 jit_solution(18231923940388810683)
XLA Ops:
  1.3 100.2 %shard_map.85 = (f32[32,512]{1,0:T(8,128)}, f32[8,128]{1,0:T(8,128)}, bf16[128,512]{1,0:T(8,128)(2,1)}) custom-call(s32[1]{0:T(128)S(6)} %copy.9.len_ref, bf16[128,8192]{1,0:T(8,128)(2,1)} %bitcast.5, bf16[8192,512]{1,0:T(8,128)(2,1)} %w_ref.1, bf16[128,4096]{1,0:T(8,128)(2,1)} %bitcast.6, bf16[128,512]{1,0:T(8,128)(2,1)} %bitcast.8, bf16[128,4096]{1,0:T(8,128)(2,1)} %bitcast.7), custom_call_target="tpu_custom_call" | custom-call | tf_op jit(solution)/shard_map/pallas_call | solution.py:393
  101.5 1.6 %shard_map.86 = (f32[32,512]{1,0:T(8,128)}, f32[1]{0:T(128)}, bf16[1,128,512]{2,1,0:T(8,128)(2,1)}) custom-call(f32[32,512]{1,0:T(8,128)} %get-tuple-element.9.clipped_ref, f32[8,128]{1,0:T(8,128)} %get-tuple-element.10.norm_ref, bf16[128,512]{1,0:T(8,128)(2,1)} %get-tuple-element.11.key_ref), custom_call_target="tpu_custom_call" | custom-call | tf_op jit(solution)/shard_map/pallas_call | solution.py:443

commit v4 on v3

--- a/solution.py
+++ b/solution.py
@@ -27,7 +27,8 @@
 KS = 512
 STEPS = CK // KS
 DB = D // NC
-DH = DB // 2
+NH = 1
+DH = DB // NH
 CB = KV // ND
 WCH = 8
 SCALE = HD ** (-0.5)
@@ -38,6 +39,7 @@
 K2, V2, XY, XX, AXF, AYF, GR, FC, RV, NM = range(32, 32 + 10 * 32, 32)
 NSEM = 352
 LX, LQ, LG, LK, LV, LXG, LW = 0, 1, 2, 3, 4, 5, 13
+
 
 def attend(k, y, length, qb, gb, kf, vf, dk, dv, qs, gs, qt, gt, p_s, d_s, m_s, done):
     q_pos = CK * k + ROWS * y + lax.broadcasted_iota(jnp.int32, (ROWS, HD), 0)
@@ -91,6 +93,7 @@
 
     lax.fori_loop(0, (k + 1) * STEPS, sweep_b, 0)
 
+
 def kernel(
     len_ref, x_ref, w_ref, q_ref, k_ref, g_ref,
     cs_ref, nm_ref, kg_ref,
@@ -144,7 +147,7 @@
     def input_cols(h, there):
         return x_ref.at[:, pl.ds(pl.multiple_of(there * DB + h * DH, DH), DH)]
 
-    for h in range(2):
+    for h in range(NH):
         for i in range(NX):
             src = input_cols(h, at_x(i) * NY + y)
             own.append(near(src, staged(h, i, y), LXG + NX * h + i))
@@ -196,9 +199,8 @@
     def grads_x(o):
         gc[o] = remote(g_ref.at[:, cols(at_x(o), GW)], gb.at[x], G + o, **on_x(o))
 
-    for o in (1, 3, 2):
-        queries_x(o)
-        grads_x(o)
+    queries_x(1)
+    queries_x(3)
 
     def gather_y(ref, sem):
         copies = []
@@ -218,6 +220,10 @@
     for copy in v1:
         copy.wait_recv()
     v2 = gather_y(vf, V2)
+    grads_x(1)
+    grads_x(3)
+    queries_x(2)
+    grads_x(2)
 
     xy, xx = {}, {}
 
@@ -238,8 +244,6 @@
         input_y(0, i)
     for copy in k2 + v2:
         copy.wait_recv()
-    for i in (1, 3, 2, 0):
-        input_y(1, i)
     def sum_copy(o, j):
         sem = RV + NX * o + j
         return pltpu.make_async_remote_copy(
@@ -293,8 +297,6 @@
 
     rv = [sum_copy(o, j) for j in range(NX) for o in range(1, NY)]
     sent.extend(rv)
-    input_x(1, 1)
-    input_x(1, 3)
     for copy in rv:
         copy.wait_recv()
     for j in range(NX):
@@ -314,12 +316,11 @@
         part = dvt.at[lax.rem(y + NY - o, NY), cols(x, HD), :half]
         for i in (1, 3, 2):
             axf[i, o] = remote(part, part, AXF + NY * i + o, **on_x(i))
-    input_x(1, 2)
     rk = split_y(dk, dks, dkr, RK, SCALE)
 
     squares = jnp.zeros((1, 1), F32)
     gx = []
-    for h in range(2):
+    for h in range(NH):
         input_x(h, 0)
         for i in range(1, NX):
             xx[h, i].wait_recv()
@@ -372,7 +373,7 @@
 
     for copy in fx + gx:
         copy.wait_recv()
-    for h in range(2):
+    for h in range(NH):
         clipped = fr[0][0:1, 0:1] * gr[h, 0].astype(F32)
         for i in range(1, ND):
             clipped = clipped + fr[i][0:1, 0:1] * gr[h, i].astype(F32)
@@ -381,10 +382,12 @@
     for copy in sent:
         copy.wait_send()
 
+
 def finish(clipped_ref, norm_ref, key_ref, cs_ref, nm_ref, kg_ref):
     cs_ref[...] = clipped_ref[...]
     nm_ref[0] = norm_ref[0, 0]
     kg_ref[0] = key_ref[...]
+
 
 def body(layer_input, value_weight, queries, key_states, out_grads, lengths):
     vm = pltpu.VMEM
@@ -407,8 +410,8 @@
             vm((NX, ROWS, GW), BF),
             vm((SEQ, HD), BF),
             vm((SEQ, HD), BF),
-            vm((2, NY, NX, ROWS, DH), BF),
-            vm((2, NX - 1, NY, ROWS, DH), BF),
+            vm((NH, NY, NX, ROWS, DH), BF),
+            vm((NH, NX - 1, NY, ROWS, DH), BF),
             vm((SEQ, HD), F32),
             vm((SEQ, HD), F32),
             vm((GW, HD), BF),
@@ -426,8 +429,8 @@
             vm((NX, ROWS, HD), BF),
             vm((NY, KV, CK), BF),
             vm((KV, DH), F32),
-            vm((2, ND, CB, DH), BF),
-            vm((2, ND, CB, DH), BF),
+            vm((NH, ND, CB, DH), BF),
+            vm((NH, ND, CB, DH), BF),
             vm((8, 128), F32),
             vm((NC, 8, 128), F32),
             vm((8, 128), F32),
@@ -452,6 +455,7 @@
     )(clipped, norm, key_grads)
     return clipped.T, norm, key_grads
 
+
 def solution(mesh):
     placed = (
         P("dp", "context", None),

time: 103 us -> 108 us (1.049)
  Pallas kernels: 102 us -> 106 us
    pallas_call x1, Pallas kernels: 100 us -> 105 us  [body(): pl.pallas_call(kernel, out_shape=(jax.ShapeDtypeStruct((CB, DB), F32), ja...]
where the time goes in v4:
time: 108 us
  Pallas kernels  106 us (98%)
  between operations  1.45 us (1%)
    pallas_call x1, Pallas kernels, body(): pl.pallas_call(kernel, out_shape=(jax.ShapeDtypeStruct((CB, DB), F32), ja...  105 us

profile of v4, /device:TPU:1, one launch (start us, length us, event | category | flops | bytes accessed | tf_op | source)
XLA Modules:
  0.0 107.7 jit_solution(13728095855625206381)
XLA Ops:
  1.3 104.6 %shard_map.85 = (f32[32,512]{1,0:T(8,128)}, f32[8,128]{1,0:T(8,128)}, bf16[128,512]{1,0:T(8,128)(2,1)}) custom-call(s32[1]{0:T(128)S(6)} %copy.9.len_ref, bf16[128,8192]{1,0:T(8,128)(2,1)} %bitcast.5, bf16[8192,512]{1,0:T(8,128)(2,1)} %w_ref.1, bf16[128,4096]{1,0:T(8,128)(2,1)} %bitcast.6, bf16[128,512]{1,0:T(8,128)(2,1)} %bitcast.8, bf16[128,4096]{1,0:T(8,128)(2,1)} %bitcast.7), custom_call_target="tpu_custom_call" | custom-call | tf_op jit(solution)/shard_map/pallas_call | solution.py:396
  105.9 1.6 %shard_map.86 = (f32[32,512]{1,0:T(8,128)}, f32[1]{0:T(128)}, bf16[1,128,512]{2,1,0:T(8,128)(2,1)}) custom-call(f32[32,512]{1,0:T(8,128)} %get-tuple-element.9.clipped_ref, f32[8,128]{1,0:T(8,128)} %get-tuple-element.10.norm_ref, bf16[128,512]{1,0:T(8,128)(2,1)} %get-tuple-element.11.key_ref), custom_call_target="tpu_custom_call" | custom-call | tf_op jit(solution)/shard_map/pallas_call | solution.py:446
